TPU v7x, 256 devices: a whole 4x4x8 slice. The times are simulated.
256 devices in a mesh: section: 2 (over core), row: 16 (over y, x), col: 8 (over z).
Axes of the slice: x: 4, y: 4, z: 8, core: 2. Of those that a mesh axis runs over, the one named last changes fastest.
Arguments:
- tables: bfloat16 [32, 4096, 256], P('col', ('section', 'row')), may hold values from -1.5 to 1.5
- bag_index: int32 [1024, 32, 32], P(None, 'col'), may hold values from 0 to 4096, as said below
- cross_weight: bfloat16 [2, 8192, 8192], P(None, 'col', ('section', 'row')), may hold values from -0.0625 to 0.0625
- cross_bias: float32 [2, 8192], replicated, may hold values from -3 to 3
- upstream: bfloat16 [1024, 8192], P(('section', 'row'), 'col'), may hold values from -6 to 6
Outputs:
- crossed: bfloat16 [1024, 8192], P(('section', 'row'), 'col')
- pooled_grad: float32 [1024, 8192], P(('section', 'row'), 'col')
- table_grad: float32 [32, 4096, 256], P('col', ('section', 'row'))
- weight_grad: float32 [2, 8192, 8192], P(None, 'col', ('section', 'row'))
- bias_grad: float32 [2, 8192], P(None, ('section', 'row'))
Inputs may be any that keep to these rules, and one draw needn't show every extreme that they name: `bag_index`: each bag lists 1 to 32 table rows first, then only the padding value 4096, which stands for a zero row.
All inputs are finite; a program needn't handle non-finite values.
Results may differ from a plain program's by a relative error of at most 0.012.
Values may be sent and summed in bfloat16 or wider, within the bound.
No kernel may reach another device: no remote copies, remote signals or barrier semaphores. Data moves between devices by JAX's collectives and lax.ppermute only.
A program may use at most 64 MiB of HBM per device.

v0:
```python
import jax
import jax.numpy as jnp
from jax import lax
from jax.experimental import pallas as pl
from jax.experimental.pallas import tpu as pltpu
from jax.sharding import Mesh, PartitionSpec as P

NS, NY, NX, NZ = 2, 4, 4, 8
BF = jnp.bfloat16
F32 = jnp.float32
VMEM_LIMIT = 16 * 1024 * 1024
NN = (((1,), (0,)), ((), ()))
NT = (((1,), (1,)), ((), ()))
TN = (((0,), (0,)), ((), ()))


def dot(left, right, dims):
    return lax.dot_general(left, right, dims, preferred_element_type=F32)


def turned(place, shift):
    return lax.rem(place + shift + 4, 4)


def other_core(value):
    return lax.ppermute(value, "s", [(0, 1), (1, 0)])


def shift_in(axis, value, k):
    return lax.ppermute(value, axis, [(i, (i + k) % 4) for i in range(4)])


def swap(axis, pieces):
    return lax.all_to_all(pieces, axis, 0, 0, tiled=True)


SCALARS = pl.BlockSpec(memory_space=pltpu.SMEM)
FREE = pl.BlockSpec(memory_space=pl.ANY)


def whole(shape):
    return pl.BlockSpec(shape, lambda i: (0,) * len(shape))


def call(kernel, ins, outs, earlier=(), name=None):
    specs = [spec if spec is not None else whole(v.shape) for v, spec in ins]
    return pl.pallas_call(
        kernel,
        grid=(1,),
        in_specs=specs + [FREE] * len(earlier),
        out_specs=[whole(v.shape) for v in outs],
        out_shape=outs,
        compiler_params=pltpu.CompilerParams(vmem_limit_bytes=VMEM_LIMIT),
        name=name,
    )(*[v for v, _ in ins], *earlier)


def nothing_kernel(*refs):
    pass


def after(value, *earlier):
    return pl.pallas_call(
        nothing_kernel,
        in_specs=[FREE] * (1 + len(earlier)),
        out_specs=FREE,
        out_shape=like(value.shape, value.dtype),
        input_output_aliases={0: 0},
        name="after",
    )(value, *earlier)


def like(shape, kind=BF):
    return jax.ShapeDtypeStruct(shape, kind)


def count_kernel(ids_ref, counts_ref):
    bag_len, rows = ids_ref.shape[1:]
    slots = counts_ref.shape[1]
    lanes = 128
    for first in range(0, rows, lanes):
        slot_ids = lax.broadcasted_iota(jnp.int32, (slots, lanes), 0).astype(F32).astype(BF)
        total = jnp.zeros((slots, lanes), BF)
        for position in range(bag_len):
            wanted = ids_ref[0, position : position + 1, first : first + lanes]
            wanted = jnp.broadcast_to(wanted, (slots, lanes)).astype(BF)
            total = total + jnp.where(wanted == slot_ids, jnp.ones((), BF), jnp.zeros((), BF))
        counts_ref[0, :, first : first + lanes] = total


def count(ids, slots):
    feats, bag_len, rows = ids.shape
    one = lambda f: (f, 0, 0)
    return pl.pallas_call(
        count_kernel,
        grid=(feats,),
        in_specs=[pl.BlockSpec((1, bag_len, rows), one)],
        out_specs=pl.BlockSpec((1, slots, rows), one),
        out_shape=like((feats, slots, rows)),
        compiler_params=pltpu.CompilerParams(vmem_limit_bytes=VMEM_LIMIT),
        name="count",
    )(ids)


def pool_kernel(at_ref, counts_ref, own_ref, other_ref, *refs):
    feats, slots, rows = counts_ref.shape
    half = slots // 2
    for k, out_ref in enumerate(refs[-feats:]):
        feat = turned(at_ref[0], k)
        summed = dot(own_ref[feat], counts_ref[feat, :half, :], TN)
        summed += dot(other_ref[feat], counts_ref[feat, half:, :], TN)
        out_ref[...] = summed.astype(BF)


def pool(at, counts, own_table, other_table, *earlier):
    feats, _, rows = counts.shape
    return call(
        pool_kernel,
        [(at, SCALARS), (counts, None), (own_table, None), (other_table, None)],
        [like((own_table.shape[2], rows))] * feats,
        earlier,
        "pool",
    )


def forward_kernel(at_ref, *refs):
    x_refs, w_refs, (out_ref, keep_ref) = refs[:NX], refs[NX : NX + 2], refs[-2:]
    width = x_refs[0].shape[0]
    s = at_ref[2]
    for u, w_ref in enumerate(w_refs):
        weight = w_ref[:, 0]
        weight_shape = (weight.shape[0] * weight.shape[1], width)
        total = None
        for k, x_ref in enumerate(x_refs):
            part = turned(at_ref[0], -k)
            block = pl.multiple_of(part * width, width)
            if u == 0:
                keep_ref[part] = x_ref[...]
            weight = w_ref[:, 0, :, pl.ds(block, width)].reshape(weight_shape)
            product = dot(weight, x_ref[...], NN)
            total = product if total is None else total + product
        total = total.astype(BF).reshape((NY, -1, total.shape[1]))
        first = NY * (s if u == 0 else 1 - s)
        for y in range(NY):
            out_ref[first + y] = total[y]


def of_layer(weights, layer):
    parts, layers, rows, columns = weights.shape
    return pl.BlockSpec((parts, 1, rows, columns), lambda i: (0, layer, 0, 0))


def forward_product(at, x_full, own_weight, other_weight, layer, *earlier):
    width, rows = x_full[0].shape
    return call(
        forward_kernel,
        [(at, SCALARS)]
        + [(v, None) for v in x_full]
        + [(v, of_layer(v, layer)) for v in (own_weight, other_weight)],
        [like((NZ, own_weight.shape[2], rows)), like((NX, width, rows))],
        earlier,
        "forward_product",
    )


def backward_kernel(at_ref, d_ref, own_ref, other_ref, *refs):
    out_refs = refs[-NX:]
    width, rows = out_refs[0].shape
    s = at_ref[2]
    firsts = (NY * s, NY * (1 - s))
    deltas = [
        jnp.concatenate([d_ref[first + y] for y in range(NY)], axis=0) for first in firsts
    ]
    for k, out_ref in enumerate(out_refs):
        block = pl.multiple_of(turned(at_ref[0], k) * width, width)
        total = None
        for delta, w_ref in zip(deltas, (own_ref, other_ref)):
            weight = w_ref[:, 0, :, pl.ds(block, width)].reshape((delta.shape[0], width))
            product = dot(weight, delta, TN)
            total = product if total is None else total + product
        out_ref[...] = total.astype(BF)


def backward_product(at, d_full, own_weight, other_weight, layer, *earlier):
    width, rows = own_weight.shape[3] // NX, d_full.shape[2]
    return call(
        backward_kernel,
        [(at, SCALARS), (d_full, None)]
        + [(v, of_layer(v, layer)) for v in (own_weight, other_weight)],
        [like((width, rows))] * NX,
        earlier,
        "backward_product",
    )


def weight_kernel(x_ref, d_ref, *refs):
    own_ref, other_ref, own_bias_ref, other_bias_ref = refs[-4:]
    columns, rows = own_ref.shape[1], x_ref.shape[2]
    deltas = [d_ref[:, 1 + u].reshape((columns, rows)) for u in range(2)]
    for delta, out_ref in zip(deltas, (own_ref, other_ref)):
        out_ref[...] = dot(x_ref[0], delta, NT)

    @pl.when(pl.program_id(0) == 0)
    def _():
        ones = jnp.ones((8, rows), BF)
        for delta, bias_ref in zip(deltas, (own_bias_ref, other_bias_ref)):
            bias_ref[...] = dot(ones, delta, NT)


def weight_product(x_keep, d_parts, *earlier):
    parts, width, rows = x_keep.shape
    columns = NY * d_parts.shape[2]
    out, bias = like((parts * width, columns), F32), like((8, columns), F32)
    block = pl.BlockSpec((width, columns), lambda i: (i, 0))
    return pl.pallas_call(
        weight_kernel,
        grid=(parts,),
        in_specs=[pl.BlockSpec((1, width, rows), lambda i: (i, 0, 0)), whole(d_parts.shape)]
        + [FREE] * len(earlier),
        out_specs=[block, block, whole(bias.shape), whole(bias.shape)],
        out_shape=[out, out, bias, bias],
        compiler_params=pltpu.CompilerParams(vmem_limit_bytes=VMEM_LIMIT),
        name="weight_product",
    )(x_keep, d_parts, *earlier)


def add_with_kernel(at_ref, d_ref, *refs):
    parts, out_ref = refs[:NX], refs[-1]
    total = parts[0][...].astype(F32)
    for ref in parts[1:]:
        total = total + ref[...].astype(F32)
    _, kinds, piece, _ = out_ref.shape
    total = total.astype(BF)
    s = at_ref[2]
    for y in range(NY):
        out_ref[y, 0] = total[y * piece : (y + 1) * piece]
        out_ref[y, 1] = d_ref[NY * s + y]
        out_ref[y, 2] = d_ref[NY * (1 - s) + y]
        if kinds == 4:
            out_ref[y, 3] = refs[NX][...]


def add_with(at, d_full, parts, following, *earlier):
    _, piece, rows = d_full.shape
    ins = [(at, SCALARS), (d_full, None)] + [(v, None) for v in parts + following]
    out = like((NY, 3 + len(following), piece, rows))
    return call(add_with_kernel, ins, [out], earlier, "add_with")[0]


def add_kernel(*refs):
    total = refs[0][...].astype(F32)
    for ref in refs[1:NX]:
        total = total + ref[...].astype(F32)
    refs[-1][...] = total.astype(BF)


def add_parts(parts, *earlier):
    return call(add_kernel, [(v, None) for v in parts], [like(parts[0].shape)], earlier, "add_parts")[0]


def collect_kernel(at_ref, *refs):
    piece = refs[0].shape[0]
    for j in range(NY):
        place = pl.multiple_of(turned(at_ref[1], -j) * piece, piece)
        refs[-1][pl.ds(place, piece), :] = refs[j][...]


def collect(at, pieces):
    piece, rows = pieces[0].shape
    ins = [(at, SCALARS)] + [(v, None) for v in pieces]
    return call(collect_kernel, ins, [like((NY * piece, rows))], name="collect")[0]


def stack_kernel(at_ref, *refs):
    for j in range(NY):
        refs[-1][turned(at_ref[1], -j)] = refs[j][...]


def stack_from(at, pieces):
    ins = [(at, SCALARS)] + [(v, None) for v in pieces]
    return call(stack_kernel, ins, [like((NY,) + pieces[0].shape)], name="stack_from")[0]


def spread_kernel(*refs):
    for at in range(refs[-1].shape[0]):
        refs[-1][at] = refs[0][...]


def spread(piece, count, *earlier):
    return call(spread_kernel, [(piece, None)], [like((count,) + piece.shape)], earlier, "spread")[0]


def pack_kernel(g_ref, last_ref, *refs):
    out_ref = refs[-1]
    rows = g_ref.shape[1]
    strip = rows // NY
    for place in range(NX * NY):
        out_ref[place, :, :rows] = g_ref[...]
        first = (place % NY) * strip
        out_ref[place, :, rows:] = last_ref[:, first : first + strip]


def pack(g, last, *earlier):
    home, rows = g.shape
    out = like((NX * NY, home, rows + rows // NY))
    return call(pack_kernel, [(g, None), (last, None)], [out], earlier, "pack")[0]


def table_kernel(counts_ref, g_ref, *refs):
    own_ref, other_ref = refs[-2:]
    feats, slots, rows = counts_ref.shape
    half = slots // 2
    for feat in range(feats):
        grads = g_ref[feat * NY : (feat + 1) * NY, :, :rows].reshape((-1, rows))
        other_ref[feat] = dot(counts_ref[feat, half:, :], grads, NT)
        own_ref[feat] = dot(counts_ref[feat, :half, :], grads, NT)


def table_product(counts, arrived, *earlier):
    feats, slots, _ = counts.shape
    out = like((feats, slots // 2, NY * arrived.shape[1]), F32)
    return call(table_kernel, [(counts, None), (arrived, None)], [out, out], earlier, "table_product")


def scatter_in_x(parts):
    return [parts[0]] + [shift_in("x", parts[k], k) for k in range(1, NX)]


def scatter_in_y(parts, *earlier):
    summed = add_parts(parts, *earlier)
    arrived = swap("y", summed.reshape((NY, -1, summed.shape[1])))
    return jnp.sum(arrived.astype(F32), axis=0)


def gather_in_y(at, piece):
    return collect(at, [piece] + [shift_in("y", piece, j) for j in range(1, NY)])


def gather_in_x(block):
    return [block] + [shift_in("x", block, k) for k in range(1, NX)]


def body(tables, bag_index, cross_weight, cross_bias, upstream):
    feats, shard, width = tables.shape
    layers, in_width, out_width = cross_weight.shape
    half_rows = bag_index.shape[0] // NS
    my_rows = upstream.shape[0]
    home = width // NY
    s, y, x, z = (lax.axis_index(name) for name in ("s", "y", "x", "z"))
    chip = y * NX + x
    at = jnp.stack([x, y, s]).astype(jnp.int32)

    other_table = other_core(tables)
    turned_weight = jnp.transpose(cross_weight.reshape(layers, in_width, NY, home), (2, 0, 3, 1))
    pick = lambda k: lax.dynamic_index_in_dim(turned_weight, turned(y, k), 0, keepdims=False)
    own_weight = stack_from(at, [pick(0)] + [shift_in("y", pick(k), k) for k in range(1, NY)])
    other_weight = other_core(own_weight)
    sent = jnp.transpose(upstream.reshape(my_rows, NX * NY, home), (1, 0, 2))
    swapped = swap(("x", "y"), sent)
    g = jnp.transpose(swapped.reshape(NX, NY, my_rows, home), (3, 1, 0, 2))
    g = g.reshape(home, half_rows).astype(F32)

    mine = lax.dynamic_slice_in_dim(bag_index, s * half_rows, half_rows, 0)
    mine = jnp.transpose(mine, (1, 2, 0))
    own_id = mine - (s * NY * NX + chip) * shard
    other_id = mine - ((1 - s) * NY * NX + chip) * shard
    own_fits = (own_id >= 0) & (own_id < shard)
    other_fits = (other_id >= 0) & (other_id < shard)
    slot = jnp.where(own_fits, own_id, jnp.where(other_fits, other_id + shard, -1))
    counts = count(slot.astype(F32), 2 * shard)
    pooled_parts = pool(at, counts, tables, other_table)

    pooled = scatter_in_y(scatter_in_x(pooled_parts), own_weight, swapped).astype(BF)
    pooled_wide = pooled.astype(F32)
    bias = lax.dynamic_slice(cross_bias, (0, z * in_width + x * width + y * home), (layers, home))

    current = pooled
    x_keeps, d_parts = [None] * layers, [None] * layers
    mixed, held = [], [None] * layers
    for step in range(layers):
        layer, back_layer = step, layers - 1 - step
        delta = (pooled_wide * g).astype(BF)
        d_full = swap("z", spread(delta, NZ))
        if step == 0:
            block = gather_in_y(at, current)
        x_full = gather_in_x(block)
        partial, x_keeps[layer] = forward_product(at, x_full, own_weight, other_weight, layer)
        partial = after(partial, d_full)
        back = backward_product(at, d_full, own_weight, other_weight, back_layer, x_keeps[layer])
        back = scatter_in_x(back)
        held[back_layer] = g
        product = swap("z", partial)
        summed = jnp.sum(product.astype(F32), axis=0)
        mixed.append(summed + bias[layer][:, None])
        current = (pooled_wide * mixed[layer] + current.astype(F32)).astype(BF)
        if step < layers - 1:
            sent = add_with(at, d_full, back, [current])
        else:
            late_grads = weight_product(x_keeps[layer], d_parts[layer], back[1])
            sent = add_with(at, d_full, back, [], product, late_grads[0])
        d_parts[back_layer] = swap("y", sent)
        g = g + jnp.sum(d_parts[back_layer][:, 0].astype(F32), axis=0)
        if step < layers - 1:
            block = d_parts[back_layer][:, 3].reshape(width, half_rows)
    for layer in range(layers):
        g = g + held[layer] * mixed[layer]
    packed = pack(g.astype(BF), current)
    arrived = swap(("x", "y"), packed)

    weight_grads, bias_grads = [None] * layers, [None] * layers
    for layer in reversed(range(layers)):
        if layer == layers - 1:
            own, other, own_bias, other_bias = late_grads
        else:
            own, other, own_bias, other_bias = weight_product(x_keeps[layer], d_parts[layer], packed)
        weight_grads[layer] = own + other_core(other)
        bias_grads[layer] = (own_bias + other_core(other_bias))[0]
    weight_grad, bias_grad = jnp.stack(weight_grads), jnp.stack(bias_grads)
    own, other = table_product(counts, arrived)
    table_grad = own + other_core(other)

    strip = half_rows // NY

    def my_part(first):
        part = lax.dynamic_slice(arrived, (0, 0, first), (NX * NY, home, my_rows))
        return jnp.transpose(part, (2, 0, 1)).reshape(my_rows, in_width)

    crossed = my_part(half_rows + x * my_rows)
    pooled_grad = my_part(y * strip + x * my_rows).astype(F32)
    return crossed, pooled_grad, table_grad, weight_grad, bias_grad


def solution(mesh):
    fine = Mesh(mesh.devices.reshape(NS, NY, NX, NZ), ("s", "y", "x", "z"))
    rows = ("s", "y", "x")
    return jax.shard_map(
        body,
        mesh=fine,
        in_specs=(
            P("z", rows, None),
            P(None, "z", None),
            P(None, "z", rows),
            P(),
            P(rows, "z"),
        ),
        out_specs=(
            P(rows, "z"),
            P(rows, "z"),
            P("z", rows, None),
            P(None, "z", rows),
            P(None, rows),
        ),
        check_vma=False,
    )
```

profile of v0, /device:TPU:1, one launch (start us, length us, event | category | flops | bytes accessed | tf_op | source)
XLA Modules:
  0.0 216.5 jit_solution(14974969170160120424)
XLA Ops:
  0.6 3.3 %collective-permute-start = (bf16[4,128,256]{2,1,0:T(8,128)(2,1)}, bf16[4,128,256]{2,1,0:T(8,128)(2,1)S(1)}, u32[]{:S(2)}, u32[]{:S(2)}) collective-permute-start(bf16[4,128,256]{2,1,0:T(8,128)(2,1)} %own_ref.1), channel_id=1, source_target_pairs={{0,128},{128,0},{1,129},{129,1},{2,130},{130,2},{3,131},{131,3},{4... | collective-permute-start | bytes 786440 | tf_op jit(solution)/shard_map/ppermute | solution.py:26
  6.3 2.2 %collective-permute-start.5 = (bf16[2,64,1024]{2,1,0:T(8,128)(2,1)S(1)}, bf16[2,64,1024]{2,1,0:T(8,128)(2,1)S(1)}, u32[]{:S(2)}, u32[]{:S(2)}) collective-permute-start(bf16[2,64,1024]{2,1,0:T(8,128)(2,1)S(1)} %get-tuple-element.72), channel_id=1, source_target_pairs={{0,64},{32,96},{64,0},{96,32},{1,65},{33,97},{65,1},{97,33},{2,66}... | collective-permute-start | bytes 786440 | tf_op jit(solution)/shard_map/ppermute | solution.py:30
  10.6 3.5 %count.1.counts_ref = bf16[4,256,512]{2,1,0:T(8,128)(2,1)S(1)} custom-call(f32[4,32,512]{2,1,0:T(8,128)S(1)} %fusion.ids_ref), custom_call_target="tpu_custom_call" | custom-call | tf_op jit(solution)/shard_map/count/pallas_call | solution.py:94
  18.1 2.5 %collective-permute-start.2 = (bf16[256,512]{1,0:T(8,128)(2,1)}, bf16[256,512]{1,0:T(8,128)(2,1)}, u32[]{:S(2)}, u32[]{:S(2)}) collective-permute-start(bf16[256,512]{1,0:T(8,128)(2,1)} %get-tuple-element.33), channel_id=1, source_target_pairs={{0,16},{8,24},{16,0},{24,8},{1,17},{9,25},{17,1},{25,9},{2,18},{10... | collective-permute-start | bytes 786440 | tf_op jit(solution)/shard_map/ppermute | solution.py:30
  22.1 11.4 %all_to_all.45 = bf16[16,2,1024]{2,1,0:T(2,128)(2,1)S(1)} all-to-all(bf16[16,2,1024]{2,1,0:T(2,128)(2,1)S(1)} %reshape.42), channel_id=1, replica_groups=mesh['s'=2,'y'=4,'x'=4,'z'=8] {'x','y'}, dimensions={0} | all-to-all | bytes 131072 | tf_op jit(solution)/shard_map/all_to_all | solution.py:34
  36.5 4.0 %all-to-all-start.1 = ((bf16[4,64,512]{2,1,0:T(8,128)(2,1)}), bf16[4,64,512]{2,1,0:T(8,128)(2,1)}, u32[]{:S(2)}, u32[]{:S(2)}) async-start(bf16[4,64,512]{2,1,0:T(8,128)(2,1)} %bitcast.18), calls=%async_computation.1 | async-start | bytes 524288 | tf_op jit(solution)/shard_map/all_to_all | solution.py:34
  42.6 3.6 %all-to-all-done.1 = bf16[4,64,512]{2,1,0:T(8,128)(2,1)} async-done(((bf16[4,64,512]{2,1,0:T(8,128)(2,1)}), bf16[4,64,512]{2,1,0:T(8,128)(2,1)}, u32[]{:S(2)}, u32[]{:S(2)}) %all-to-all-start.1) | async-done | bytes 262176 | tf_op jit(solution)/shard_map/all_to_all | solution.py:34
  48.0 7.0 %all-to-all-start.2 = ((bf16[8,64,512]{2,1,0:T(8,128)(2,1)}), bf16[8,64,512]{2,1,0:T(8,128)(2,1)}, u32[]{:S(2)}, u32[]{:S(2)}) async-start(bf16[8,64,512]{2,1,0:T(8,128)(2,1)} %copy-done.12), calls=%async_computation.2 | async-start | bytes 1048576 | tf_op jit(solution)/shard_map/all_to_all | solution.py:34
  58.2 2.1 collective-permute-done.8.refs_1_
  63.5 3.4 %collective-permute-start.12 = (bf16[256,512]{1,0:T(8,128)(2,1)S(1)}, bf16[256,512]{1,0:T(8,128)(2,1)S(1)}, u32[]{:S(2)}, u32[]{:S(2)}) collective-permute-start(bf16[256,512]{1,0:T(8,128)(2,1)S(1)} %collect.1.refs_0_), channel_id=1, source_target_pairs={{0,16},{8,24},{16,0},{24,8},{1,17},{9,25},{17,1},{25,9},{2,18},{10... | collective-permute-start | bytes 786440 | tf_op jit(solution)/shard_map/ppermute | solution.py:30
  66.9 2.6 %collective-permute-done.11.refs_1_ = bf16[256,512]{1,0:T(8,128)(2,1)S(1)} collective-permute-done((bf16[256,512]{1,0:T(8,128)(2,1)S(1)}, bf16[256,512]{1,0:T(8,128)(2,1)S(1)}, u32[]{:S(2)}, u32[]{:S(2)}) %collective-permute-start.11) | collective-permute-done | bytes 262176 | tf_op jit(solution)/shard_map/ppermute | solution.py:30
  69.5 5.5 %collective-permute-done.12.refs_2_ = bf16[256,512]{1,0:T(8,128)(2,1)S(1)} collective-permute-done((bf16[256,512]{1,0:T(8,128)(2,1)S(1)}, bf16[256,512]{1,0:T(8,128)(2,1)S(1)}, u32[]{:S(2)}, u32[]{:S(2)}) %collective-permute-start.12) | collective-permute-done | bytes 262176 | tf_op jit(solution)/shard_map/ppermute | solution.py:30
  78.1 6.7 %all-to-all-start.3 = ((bf16[8,64,512]{2,1,0:T(8,128)(2,1)}), bf16[8,64,512]{2,1,0:T(8,128)(2,1)}, u32[]{:S(2)}, u32[]{:S(2)}) async-start(bf16[8,64,512]{2,1,0:T(8,128)(2,1)} %after.2), calls=%async_computation.3 | async-start | bytes 1048576 | tf_op jit(solution)/shard_map/all_to_all | solution.py:34
  86.2 2.5 %backward_product.2 = (bf16[256,512]{1,0:T(8,128)(2,1)S(1)}, bf16[256,512]{1,0:T(8,128)(2,1)}, bf16[256,512]{1,0:T(8,128)(2,1)}, bf16[256,512]{1,0:T(8,128)(2,1)}) custom-call(s32[3]{0:T(128)S(1)} %pad_add_fusion.at_ref, bf16[8,64,512]{2,1,0:T(8,128)(2,1)} %all-to-all-done.2.d_ref.refs_1_, bf16[4,2,64,1024]{3,2,1,0:T(8,128)(2,1)S(1)} %stack_from.1.refs_4_.own_ref, ...), custom_call_target="tpu_custom_call" | custom-call | tf_op jit(solution)/shard_map/backward_product/pallas_call | solution.py:47
  89.4 2.7 %collective-permute-start.15 = (bf16[256,512]{1,0:T(8,128)(2,1)}, bf16[256,512]{1,0:T(8,128)(2,1)}, u32[]{:S(2)}, u32[]{:S(2)}) collective-permute-start(bf16[256,512]{1,0:T(8,128)(2,1)} %get-tuple-element.38), channel_id=1, source_target_pairs={{0,16},{8,24},{16,0},{24,8},{1,17},{9,25},{17,1},{25,9},{2,18},{10... | collective-permute-start | bytes 786440 | tf_op jit(solution)/shard_map/ppermute | solution.py:30
  92.1 4.9 %all-to-all-done.3 = bf16[8,64,512]{2,1,0:T(8,128)(2,1)} async-done(((bf16[8,64,512]{2,1,0:T(8,128)(2,1)}), bf16[8,64,512]{2,1,0:T(8,128)(2,1)}, u32[]{:S(2)}, u32[]{:S(2)}) %all-to-all-start.3) | async-done | bytes 524320 | tf_op jit(solution)/shard_map/all_to_all | solution.py:34
  102.2 13.4 %all_to_all.46.d_ref = bf16[4,4,64,512]{3,2,1,0:T(8,128)(2,1)S(1)} all-to-all(bf16[4,4,64,512]{3,2,1,0:T(8,128)(2,1)S(1)} %add_with.2), channel_id=1, replica_groups=mesh['s'=2,'y'=4,'x'=4,'z'=8] {'y'}, dimensions={0} | all-to-all | bytes 2097152 | tf_op jit(solution)/shard_map/all_to_all | solution.py:34
  118.2 6.6 %all-to-all-start.5 = ((bf16[8,64,512]{2,1,0:T(8,128)(2,1)}), bf16[8,64,512]{2,1,0:T(8,128)(2,1)}, u32[]{:S(2)}, u32[]{:S(2)}) async-start(bf16[8,64,512]{2,1,0:T(8,128)(2,1)} %copy-done.13), calls=%async_computation.5 | async-start | bytes 1048576 | tf_op jit(solution)/shard_map/all_to_all | solution.py:34
  125.9 3.1 %collective-permute-start.18 = (bf16[256,512]{1,0:T(8,128)(2,1)S(1)}, bf16[256,512]{1,0:T(8,128)(2,1)S(1)}, u32[]{:S(2)}, u32[]{:S(2)}) collective-permute-start(bf16[256,512]{1,0:T(8,128)(2,1)S(1)} %bitcast.68), channel_id=1, source_target_pairs={{0,16},{8,24},{16,0},{24,8},{1,17},{9,25},{17,1},{25,9},{2,18},{10... | collective-permute-start | bytes 786440 | tf_op jit(solution)/shard_map/ppermute | solution.py:30
  129.0 3.3 %collective-permute-done.17.refs_1_ = bf16[256,512]{1,0:T(8,128)(2,1)S(1)} collective-permute-done((bf16[256,512]{1,0:T(8,128)(2,1)S(1)}, bf16[256,512]{1,0:T(8,128)(2,1)S(1)}, u32[]{:S(2)}, u32[]{:S(2)}) %collective-permute-start.17) | collective-permute-done | bytes 262176 | tf_op jit(solution)/shard_map/ppermute | solution.py:30
  132.3 3.2 %collective-permute-done.18.refs_2_ = bf16[256,512]{1,0:T(8,128)(2,1)S(1)} collective-permute-done((bf16[256,512]{1,0:T(8,128)(2,1)S(1)}, bf16[256,512]{1,0:T(8,128)(2,1)S(1)}, u32[]{:S(2)}, u32[]{:S(2)}) %collective-permute-start.18) | collective-permute-done | bytes 262176 | tf_op jit(solution)/shard_map/ppermute | solution.py:30
  138.8 7.0 %all-to-all-start.6 = ((bf16[8,64,512]{2,1,0:T(8,128)(2,1)}), bf16[8,64,512]{2,1,0:T(8,128)(2,1)}, u32[]{:S(2)}, u32[]{:S(2)}) async-start(bf16[8,64,512]{2,1,0:T(8,128)(2,1)} %after.3), calls=%async_computation.6 | async-start | bytes 1048576 | tf_op jit(solution)/shard_map/all_to_all | solution.py:34
  149.7 3.6 %collective-permute-start.21 = (bf16[256,512]{1,0:T(8,128)(2,1)S(1)}, bf16[256,512]{1,0:T(8,128)(2,1)S(1)}, u32[]{:S(2)}, u32[]{:S(2)}) collective-permute-start(bf16[256,512]{1,0:T(8,128)(2,1)S(1)} %get-tuple-element.44), channel_id=1, source_target_pairs={{0,16},{8,24},{16,0},{24,8},{1,17},{9,25},{17,1},{25,9},{2,18},{10... | collective-permute-start | bytes 786440 | tf_op jit(solution)/shard_map/ppermute | solution.py:30
  153.3 2.9 %collective-permute-done.20.refs_0_.refs_1_ = bf16[256,512]{1,0:T(8,128)(2,1)S(1)} collective-permute-done((bf16[256,512]{1,0:T(8,128)(2,1)S(1)}, bf16[256,512]{1,0:T(8,128)(2,1)S(1)}, u32[]{:S(2)}, u32[]{:S(2)}) %collective-permute-start.20) | collective-permute-done | bytes 262176 | tf_op jit(solution)/shard_map/ppermute | solution.py:30
  161.9 3.6 %all-to-all-start.7 = ((bf16[4,3,64,512]{3,2,1,0:T(8,128)(2,1)}), bf16[4,3,64,512]{3,2,1,0:T(8,128)(2,1)S(1)}, u32[]{:S(2)}, u32[]{:S(2)}) async-start(bf16[4,3,64,512]{3,2,1,0:T(8,128)(2,1)} %copy-done.9), calls=%async_computation.7 | async-start | bytes 1572864 | tf_op jit(solution)/shard_map/all_to_all | solution.py:34
  165.6 10.9 %collective-permute-start.25 = (f32[1024,256]{1,0:T(8,128)}, f32[1024,256]{1,0:T(8,128)}, u32[]{:S(2)}, u32[]{:S(2)}) collective-permute-start(f32[1024,256]{1,0:T(8,128)} %copy-done.25), channel_id=1, source_target_pairs={{0,128},{128,0},{1,129},{129,1},{2,130},{130,2},{3,131},{131,3},{4... | collective-permute-start | bytes 3145736 | tf_op jit(solution)/shard_map/ppermute | solution.py:26
  179.8 6.6 %all-to-all-start.8 = ((bf16[16,64,640]{2,1,0:T(8,128)(2,1)}), bf16[16,64,640]{2,1,0:T(8,128)(2,1)S(1)}, u32[]{:S(2)}, u32[]{:S(2)}) async-start(bf16[16,64,640]{2,1,0:T(8,128)(2,1)} %pack.1.refs_0_), calls=%async_computation.8 | async-start | bytes 2621440 | tf_op jit(solution)/shard_map/all_to_all | solution.py:34
  187.6 2.6 %weight_product.3 = (f32[1024,256]{1,0:T(8,128)S(1)}, f32[1024,256]{1,0:T(8,128)}, f32[8,256]{1,0:T(8,128)S(1)}, f32[8,256]{1,0:T(8,128)S(1)}) custom-call(bf16[4,256,512]{2,1,0:T(8,128)(2,1)S(1)} %copy-done.5, bf16[4,3,64,512]{3,2,1,0:T(8,128)(2,1)S(1)} %all-to-all-done.7.d_ref, bf16[16,64,640]{2,1,0:T(8,128)(2,1)} %pack.1.refs_0_), custom_call_target="tpu_custom_call" | custom-call | tf_op jit(solution)/shard_map/weight_product/pallas_call | solution.py:215
  191.2 6.3 %collective-permute-start.24 = (f32[1024,256]{1,0:T(8,128)}, f32[1024,256]{1,0:T(8,128)}, u32[]{:S(2)}, u32[]{:S(2)}) collective-permute-start(f32[1024,256]{1,0:T(8,128)} %get-tuple-element.51), channel_id=1, source_target_pairs={{0,128},{128,0},{1,129},{129,1},{2,130},{130,2},{3,131},{131,3},{4... | collective-permute-start | bytes 3145736 | tf_op jit(solution)/shard_map/ppermute | solution.py:26
  197.5 2.2 collective-permute-done.27
  199.8 2.7 %add_bitcast_fusion = f32[1,1024,256]{2,1,0:T(8,128)} fusion(f32[1024,256]{1,0:T(8,128)} %copy-done.6, f32[1024,256]{1,0:T(8,128)} %collective-permute-done.25), kind=kLoop, calls=%fused_computation.1 | loop fusion | flops 262144 | bytes 3145728 | tf_op jit(solution)/shard_map/stack | solution.py:418
  205.5 4.4 %collective-permute-start.23 = (f32[4,128,256]{2,1,0:T(8,128)}, f32[4,128,256]{2,1,0:T(8,128)}, u32[]{:S(2)}, u32[]{:S(2)}) collective-permute-start(f32[4,128,256]{2,1,0:T(8,128)} %get-tuple-element.49), channel_id=1, source_target_pairs={{0,128},{128,0},{1,129},{129,1},{2,130},{130,2},{3,131},{131,3},{4... | collective-permute-start | bytes 1572872 | tf_op jit(solution)/shard_map/ppermute | solution.py:26
  (151 shorter events, 65.0 us)
Async XLA Ops:
  0.6 13.6 %collective-permute-start = (bf16[4,128,256]{2,1,0:T(8,128)(2,1)}, bf16[4,128,256]{2,1,0:T(8,128)(2,1)S(1)}, u32[]{:S(2)}, u32[]{:S(2)}) collective-permute-start(bf16[4,128,256]{2,1,0:T(8,128)(2,1)} %own_ref.1), channel_id=1, source_target_pairs={{0,128},{128,0},{1,129},{129,1},{2,130},{130,2},{3,131},{131,3},{4... | collective-permute-start | bytes 786440 | tf_op jit(solution)/shard_map/ppermute | solution.py:26
  6.3 14.3 %collective-permute-start.4 = (bf16[2,64,1024]{2,1,0:T(8,128)(2,1)}, bf16[2,64,1024]{2,1,0:T(8,128)(2,1)S(1)}, u32[]{:S(2)}, u32[]{:S(2)}) collective-permute-start(bf16[2,64,1024]{2,1,0:T(8,128)(2,1)} %get-tuple-element.73), channel_id=1, source_target_pairs={{0,32},{32,64},{64,96},{96,0},{1,33},{33,65},{65,97},{97,1},{2,34}... | collective-permute-start | bytes 786440 | tf_op jit(solution)/shard_map/ppermute | solution.py:30
  6.3 27.3 %collective-permute-start.5 = (bf16[2,64,1024]{2,1,0:T(8,128)(2,1)S(1)}, bf16[2,64,1024]{2,1,0:T(8,128)(2,1)S(1)}, u32[]{:S(2)}, u32[]{:S(2)}) collective-permute-start(bf16[2,64,1024]{2,1,0:T(8,128)(2,1)S(1)} %get-tuple-element.72), channel_id=1, source_target_pairs={{0,64},{32,96},{64,0},{96,32},{1,65},{33,97},{65,1},{97,33},{2,66}... | collective-permute-start | bytes 786440 | tf_op jit(solution)/shard_map/ppermute | solution.py:30
  8.5 25.2 %collective-permute-start.6 = (bf16[2,64,1024]{2,1,0:T(8,128)(2,1)S(1)}, bf16[2,64,1024]{2,1,0:T(8,128)(2,1)S(1)}, u32[]{:S(2)}, u32[]{:S(2)}) collective-permute-start(bf16[2,64,1024]{2,1,0:T(8,128)(2,1)S(1)} %get-tuple-element.71), channel_id=1, source_target_pairs={{0,96},{32,0},{64,32},{96,64},{1,97},{33,1},{65,33},{97,65},{2,98}... | collective-permute-start | bytes 786440 | tf_op jit(solution)/shard_map/ppermute | solution.py:30
  16.9 17.4 %collective-permute-start.1 = (bf16[256,512]{1,0:T(8,128)(2,1)}, bf16[256,512]{1,0:T(8,128)(2,1)}, u32[]{:S(2)}, u32[]{:S(2)}) collective-permute-start(bf16[256,512]{1,0:T(8,128)(2,1)} %get-tuple-element.32), channel_id=1, source_target_pairs={{0,8},{8,16},{16,24},{24,0},{1,9},{9,17},{17,25},{25,1},{2,10},{10... | collective-permute-start | bytes 786440 | tf_op jit(solution)/shard_map/ppermute | solution.py:30
  18.1 16.2 %collective-permute-start.2 = (bf16[256,512]{1,0:T(8,128)(2,1)}, bf16[256,512]{1,0:T(8,128)(2,1)}, u32[]{:S(2)}, u32[]{:S(2)}) collective-permute-start(bf16[256,512]{1,0:T(8,128)(2,1)} %get-tuple-element.33), channel_id=1, source_target_pairs={{0,16},{8,24},{16,0},{24,8},{1,17},{9,25},{17,1},{25,9},{2,18},{10... | collective-permute-start | bytes 786440 | tf_op jit(solution)/shard_map/ppermute | solution.py:30
  20.6 13.7 %collective-permute-start.3 = (bf16[256,512]{1,0:T(8,128)(2,1)}, bf16[256,512]{1,0:T(8,128)(2,1)}, u32[]{:S(2)}, u32[]{:S(2)}) collective-permute-start(bf16[256,512]{1,0:T(8,128)(2,1)} %get-tuple-element.34), channel_id=1, source_target_pairs={{0,24},{8,0},{16,8},{24,16},{1,25},{9,1},{17,9},{25,17},{2,26},{10... | collective-permute-start | bytes 786440 | tf_op jit(solution)/shard_map/ppermute | solution.py:30
  36.5 9.6 %all-to-all-start.1 = ((bf16[4,64,512]{2,1,0:T(8,128)(2,1)}), bf16[4,64,512]{2,1,0:T(8,128)(2,1)}, u32[]{:S(2)}, u32[]{:S(2)}) async-start(bf16[4,64,512]{2,1,0:T(8,128)(2,1)} %bitcast.18), calls=%async_computation.1 | async-start | bytes 524288 | tf_op jit(solution)/shard_map/all_to_all | solution.py:34
  40.7 34.3 %collective-permute-start.7 = (bf16[4,2,64,1024]{3,2,1,0:T(8,128)(2,1)S(1)}, bf16[4,2,64,1024]{3,2,1,0:T(8,128)(2,1)S(1)}, u32[]{:S(2)}, u32[]{:S(2)}) collective-permute-start(bf16[4,2,64,1024]{3,2,1,0:T(8,128)(2,1)S(1)} %stack_from.1.refs_4_.own_ref), channel_id=1, source_target_pairs={{0,128},{128,0},{1,129},{129,1},{2,130},{130,2},{3,131},{131,3},{4... | collective-permute-start | bytes 3145736 | tf_op jit(solution)/shard_map/ppermute | solution.py:26
  48.0 30.1 %all-to-all-start.2 = ((bf16[8,64,512]{2,1,0:T(8,128)(2,1)}), bf16[8,64,512]{2,1,0:T(8,128)(2,1)}, u32[]{:S(2)}, u32[]{:S(2)}) async-start(bf16[8,64,512]{2,1,0:T(8,128)(2,1)} %copy-done.12), calls=%async_computation.2 | async-start | bytes 1048576 | tf_op jit(solution)/shard_map/all_to_all | solution.py:34
  56.0 4.3 %collective-permute-start.8 = (bf16[64,512]{1,0:T(8,128)(2,1)S(1)}, bf16[64,512]{1,0:T(8,128)(2,1)S(1)}, u32[]{:S(2)}, u32[]{:S(2)}) collective-permute-start(bf16[64,512]{1,0:T(8,128)(2,1)S(1)} %reduce_sum.48.refs_0_), channel_id=1, source_target_pairs={{0,32},{32,64},{64,96},{96,0},{1,33},{33,65},{65,97},{97,1},{2,34}... | collective-permute-start | bytes 196616 | tf_op jit(solution)/shard_map/ppermute | solution.py:30
  56.5 4.6 %collective-permute-start.9 = (bf16[64,512]{1,0:T(8,128)(2,1)S(1)}, bf16[64,512]{1,0:T(8,128)(2,1)S(1)}, u32[]{:S(2)}, u32[]{:S(2)}) collective-permute-start(bf16[64,512]{1,0:T(8,128)(2,1)S(1)} %reduce_sum.48.refs_0_), channel_id=1, source_target_pairs={{0,64},{32,96},{64,0},{96,32},{1,65},{33,97},{65,1},{97,33},{2,66}... | collective-permute-start | bytes 196616 | tf_op jit(solution)/shard_map/ppermute | solution.py:30
  61.7 7.8 %collective-permute-start.11 = (bf16[256,512]{1,0:T(8,128)(2,1)S(1)}, bf16[256,512]{1,0:T(8,128)(2,1)S(1)}, u32[]{:S(2)}, u32[]{:S(2)}) collective-permute-start(bf16[256,512]{1,0:T(8,128)(2,1)S(1)} %collect.1.refs_0_), channel_id=1, source_target_pairs={{0,8},{8,16},{16,24},{24,0},{1,9},{9,17},{17,25},{25,1},{2,10},{10... | collective-permute-start | bytes 786440 | tf_op jit(solution)/shard_map/ppermute | solution.py:30
  63.5 11.5 %collective-permute-start.12 = (bf16[256,512]{1,0:T(8,128)(2,1)S(1)}, bf16[256,512]{1,0:T(8,128)(2,1)S(1)}, u32[]{:S(2)}, u32[]{:S(2)}) collective-permute-start(bf16[256,512]{1,0:T(8,128)(2,1)S(1)} %collect.1.refs_0_), channel_id=1, source_target_pairs={{0,16},{8,24},{16,0},{24,8},{1,17},{9,25},{17,1},{25,9},{2,18},{10... | collective-permute-start | bytes 786440 | tf_op jit(solution)/shard_map/ppermute | solution.py:30
  66.9 8.1 %collective-permute-start.13 = (bf16[256,512]{1,0:T(8,128)(2,1)S(1)}, bf16[256,512]{1,0:T(8,128)(2,1)S(1)}, u32[]{:S(2)}, u32[]{:S(2)}) collective-permute-start(bf16[256,512]{1,0:T(8,128)(2,1)S(1)} %collect.1.refs_0_), channel_id=1, source_target_pairs={{0,24},{8,0},{16,8},{24,16},{1,25},{9,1},{17,9},{25,17},{2,26},{10... | collective-permute-start | bytes 786440 | tf_op jit(solution)/shard_map/ppermute | solution.py:30
  78.1 18.9 %all-to-all-start.3 = ((bf16[8,64,512]{2,1,0:T(8,128)(2,1)}), bf16[8,64,512]{2,1,0:T(8,128)(2,1)}, u32[]{:S(2)}, u32[]{:S(2)}) async-start(bf16[8,64,512]{2,1,0:T(8,128)(2,1)} %after.2), calls=%async_computation.3 | async-start | bytes 1048576 | tf_op jit(solution)/shard_map/all_to_all | solution.py:34
  89.4 8.8 %collective-permute-start.14 = (bf16[256,512]{1,0:T(8,128)(2,1)}, bf16[256,512]{1,0:T(8,128)(2,1)}, u32[]{:S(2)}, u32[]{:S(2)}) collective-permute-start(bf16[256,512]{1,0:T(8,128)(2,1)} %get-tuple-element.37), channel_id=1, source_target_pairs={{0,8},{8,16},{16,24},{24,0},{1,9},{9,17},{17,25},{25,1},{2,10},{10... | collective-permute-start | bytes 786440 | tf_op jit(solution)/shard_map/ppermute | solution.py:30
  89.4 9.8 %collective-permute-start.15 = (bf16[256,512]{1,0:T(8,128)(2,1)}, bf16[256,512]{1,0:T(8,128)(2,1)}, u32[]{:S(2)}, u32[]{:S(2)}) collective-permute-start(bf16[256,512]{1,0:T(8,128)(2,1)} %get-tuple-element.38), channel_id=1, source_target_pairs={{0,16},{8,24},{16,0},{24,8},{1,17},{9,25},{17,1},{25,9},{2,18},{10... | collective-permute-start | bytes 786440 | tf_op jit(solution)/shard_map/ppermute | solution.py:30
  92.1 7.8 %collective-permute-start.16 = (bf16[256,512]{1,0:T(8,128)(2,1)}, bf16[256,512]{1,0:T(8,128)(2,1)}, u32[]{:S(2)}, u32[]{:S(2)}) collective-permute-start(bf16[256,512]{1,0:T(8,128)(2,1)} %get-tuple-element.39), channel_id=1, source_target_pairs={{0,24},{8,0},{16,8},{24,16},{1,25},{9,1},{17,9},{25,17},{2,26},{10... | collective-permute-start | bytes 786440 | tf_op jit(solution)/shard_map/ppermute | solution.py:30
  118.2 20.6 %all-to-all-start.5 = ((bf16[8,64,512]{2,1,0:T(8,128)(2,1)}), bf16[8,64,512]{2,1,0:T(8,128)(2,1)}, u32[]{:S(2)}, u32[]{:S(2)}) async-start(bf16[8,64,512]{2,1,0:T(8,128)(2,1)} %copy-done.13), calls=%async_computation.5 | async-start | bytes 1048576 | tf_op jit(solution)/shard_map/all_to_all | solution.py:34
  125.8 6.5 %collective-permute-start.17 = (bf16[256,512]{1,0:T(8,128)(2,1)S(1)}, bf16[256,512]{1,0:T(8,128)(2,1)S(1)}, u32[]{:S(2)}, u32[]{:S(2)}) collective-permute-start(bf16[256,512]{1,0:T(8,128)(2,1)S(1)} %bitcast.67), channel_id=1, source_target_pairs={{0,8},{8,16},{16,24},{24,0},{1,9},{9,17},{17,25},{25,1},{2,10},{10... | collective-permute-start | bytes 786440 | tf_op jit(solution)/shard_map/ppermute | solution.py:30
  125.9 9.6 %collective-permute-start.18 = (bf16[256,512]{1,0:T(8,128)(2,1)S(1)}, bf16[256,512]{1,0:T(8,128)(2,1)S(1)}, u32[]{:S(2)}, u32[]{:S(2)}) collective-permute-start(bf16[256,512]{1,0:T(8,128)(2,1)S(1)} %bitcast.68), channel_id=1, source_target_pairs={{0,16},{8,24},{16,0},{24,8},{1,17},{9,25},{17,1},{25,9},{2,18},{10... | collective-permute-start | bytes 786440 | tf_op jit(solution)/shard_map/ppermute | solution.py:30
  129.0 6.8 %collective-permute-start.19 = (bf16[256,512]{1,0:T(8,128)(2,1)S(1)}, bf16[256,512]{1,0:T(8,128)(2,1)S(1)}, u32[]{:S(2)}, u32[]{:S(2)}) collective-permute-start(bf16[256,512]{1,0:T(8,128)(2,1)S(1)} %bitcast.69), channel_id=1, source_target_pairs={{0,24},{8,0},{16,8},{24,16},{1,25},{9,1},{17,9},{25,17},{2,26},{10... | collective-permute-start | bytes 786440 | tf_op jit(solution)/shard_map/ppermute | solution.py:30
  138.8 21.1 %all-to-all-start.6 = ((bf16[8,64,512]{2,1,0:T(8,128)(2,1)}), bf16[8,64,512]{2,1,0:T(8,128)(2,1)}, u32[]{:S(2)}, u32[]{:S(2)}) async-start(bf16[8,64,512]{2,1,0:T(8,128)(2,1)} %after.3), calls=%async_computation.6 | async-start | bytes 1048576 | tf_op jit(solution)/shard_map/all_to_all | solution.py:34
  149.7 6.4 %collective-permute-start.20 = (bf16[256,512]{1,0:T(8,128)(2,1)S(1)}, bf16[256,512]{1,0:T(8,128)(2,1)S(1)}, u32[]{:S(2)}, u32[]{:S(2)}) collective-permute-start(bf16[256,512]{1,0:T(8,128)(2,1)S(1)} %get-tuple-element.43), channel_id=1, source_target_pairs={{0,8},{8,16},{16,24},{24,0},{1,9},{9,17},{17,25},{25,1},{2,10},{10... | collective-permute-start | bytes 786440 | tf_op jit(solution)/shard_map/ppermute | solution.py:30
  149.7 10.1 %collective-permute-start.21 = (bf16[256,512]{1,0:T(8,128)(2,1)S(1)}, bf16[256,512]{1,0:T(8,128)(2,1)S(1)}, u32[]{:S(2)}, u32[]{:S(2)}) collective-permute-start(bf16[256,512]{1,0:T(8,128)(2,1)S(1)} %get-tuple-element.44), channel_id=1, source_target_pairs={{0,16},{8,24},{16,0},{24,8},{1,17},{9,25},{17,1},{25,9},{2,18},{10... | collective-permute-start | bytes 786440 | tf_op jit(solution)/shard_map/ppermute | solution.py:30
  153.3 6.6 %collective-permute-start.22 = (bf16[256,512]{1,0:T(8,128)(2,1)S(1)}, bf16[256,512]{1,0:T(8,128)(2,1)S(1)}, u32[]{:S(2)}, u32[]{:S(2)}) collective-permute-start(bf16[256,512]{1,0:T(8,128)(2,1)S(1)} %get-tuple-element.45), channel_id=1, source_target_pairs={{0,24},{8,0},{16,8},{24,16},{1,25},{9,1},{17,9},{25,17},{2,26},{10... | collective-permute-start | bytes 786440 | tf_op jit(solution)/shard_map/ppermute | solution.py:30
  161.9 15.6 %all-to-all-start.7 = ((bf16[4,3,64,512]{3,2,1,0:T(8,128)(2,1)}), bf16[4,3,64,512]{3,2,1,0:T(8,128)(2,1)S(1)}, u32[]{:S(2)}, u32[]{:S(2)}) async-start(bf16[4,3,64,512]{3,2,1,0:T(8,128)(2,1)} %copy-done.9), calls=%async_computation.7 | async-start | bytes 1572864 | tf_op jit(solution)/shard_map/all_to_all | solution.py:34
  165.6 34.2 %collective-permute-start.25 = (f32[1024,256]{1,0:T(8,128)}, f32[1024,256]{1,0:T(8,128)}, u32[]{:S(2)}, u32[]{:S(2)}) collective-permute-start(f32[1024,256]{1,0:T(8,128)} %copy-done.25), channel_id=1, source_target_pairs={{0,128},{128,0},{1,129},{129,1},{2,130},{130,2},{3,131},{131,3},{4... | collective-permute-start | bytes 3145736 | tf_op jit(solution)/shard_map/ppermute | solution.py:26
  179.8 23.3 %all-to-all-start.8 = ((bf16[16,64,640]{2,1,0:T(8,128)(2,1)}), bf16[16,64,640]{2,1,0:T(8,128)(2,1)S(1)}, u32[]{:S(2)}, u32[]{:S(2)}) async-start(bf16[16,64,640]{2,1,0:T(8,128)(2,1)} %pack.1.refs_0_), calls=%async_computation.8 | async-start | bytes 2621440 | tf_op jit(solution)/shard_map/all_to_all | solution.py:34
  191.2 18.7 %collective-permute-start.24 = (f32[1024,256]{1,0:T(8,128)}, f32[1024,256]{1,0:T(8,128)}, u32[]{:S(2)}, u32[]{:S(2)}) collective-permute-start(f32[1024,256]{1,0:T(8,128)} %get-tuple-element.51), channel_id=1, source_target_pairs={{0,128},{128,0},{1,129},{129,1},{2,130},{130,2},{3,131},{131,3},{4... | collective-permute-start | bytes 3145736 | tf_op jit(solution)/shard_map/ppermute | solution.py:26
  205.5 9.0 %collective-permute-start.23 = (f32[4,128,256]{2,1,0:T(8,128)}, f32[4,128,256]{2,1,0:T(8,128)}, u32[]{:S(2)}, u32[]{:S(2)}) collective-permute-start(f32[4,128,256]{2,1,0:T(8,128)} %get-tuple-element.49), channel_id=1, source_target_pairs={{0,128},{128,0},{1,129},{129,1},{2,130},{130,2},{3,131},{131,3},{4... | collective-permute-start | bytes 1572872 | tf_op jit(solution)/shard_map/ppermute | solution.py:26
  (33 other events, 193.2 us)
where the time goes:
time: 218 us; the launch traced here: 216 us
  starting transfers between devices  93.3 us (43%)
  waiting for transfers between devices  35.2 us (16%)
  Pallas kernels  25 us (11%)
  blocking collectives  24.9 us (11%)
  local copies, waits for them, and re-layouts  22.5 us (10%)
  other arithmetic  14.5 us (7%)
    all_to_all x7, starting transfers between devices, swap(): return lax.all_to_all(pieces, axis, 0, 0, tiled=True)  41.7 us
    ppermute x7, starting transfers between devices, other_core(): return lax.ppermute(value, 's', [(0, 1), (1, 0)])  26.8 us
    all_to_all x2, blocking collectives, swap(): return lax.all_to_all(pieces, axis, 0, 0, tiled=True)  24.9 us
    ppermute x21, starting transfers between devices, shift_in(): return lax.ppermute(value, axis, [(i, (i + k) % 4) for i in range(4)])  24.8 us
    ppermute x21, waiting for transfers between devices, shift_in(): return lax.ppermute(value, axis, [(i, (i + k) % 4) for i in range(4)])  24.5 us
    unnamed x65, local copies, waits for them, and re-layouts  20.3 us
    pallas_call x14, Pallas kernels, call(): pl.pallas_call(kernel, grid=(1,), in_specs=specs + [FREE] * len(earlier),...  17.4 us
    all_to_all x7, waiting for transfers between devices, swap(): return lax.all_to_all(pieces, axis, 0, 0, tiled=True)  8.48 us
  transfers between devices with their start and end apart: 35, of which 15 were waited for; matrix products, arithmetic and copies ran while one was open for 8% of the time, Pallas kernels for 9%

commit v1 on v0

--- a/solution.py
+++ b/solution.py
@@ -224,6 +224,26 @@
     )(x_keep, d_parts, *earlier)
 
 
+def join_kernel(own_ref, other_ref, *refs):
+    refs[-1][0] = own_ref[...] + other_ref[...]
+
+
+def join(own, other, layer, layers, held=None):
+    out = like((layers,) + own.shape, F32)
+    place = pl.BlockSpec((1,) + own.shape, lambda i: (layer, 0, 0))
+    extra = [] if held is None else [held]
+    return pl.pallas_call(
+        join_kernel,
+        grid=(1,),
+        in_specs=[whole(own.shape)] * 2 + [FREE] * len(extra),
+        out_specs=place,
+        out_shape=out,
+        input_output_aliases={2: 0} if extra else {},
+        compiler_params=pltpu.CompilerParams(vmem_limit_bytes=VMEM_LIMIT),
+        name="join",
+    )(own, other, *extra)
+
+
 def add_with_kernel(at_ref, d_ref, *refs):
     parts, out_ref = refs[:NX], refs[-1]
     total = parts[0][...].astype(F32)
@@ -386,7 +406,7 @@
         x_full = gather_in_x(block)
         partial, x_keeps[layer] = forward_product(at, x_full, own_weight, other_weight, layer)
         partial = after(partial, d_full)
-        back = backward_product(at, d_full, own_weight, other_weight, back_layer, x_keeps[layer])
+        back = backward_product(at, d_full, own_weight, other_weight, back_layer, partial)
         back = scatter_in_x(back)
         held[back_layer] = g
         product = swap("z", partial)
@@ -407,15 +427,15 @@
     packed = pack(g.astype(BF), current)
     arrived = swap(("x", "y"), packed)
 
-    weight_grads, bias_grads = [None] * layers, [None] * layers
+    weight_grad, bias_grads = None, [None] * layers
     for layer in reversed(range(layers)):
         if layer == layers - 1:
             own, other, own_bias, other_bias = late_grads
         else:
             own, other, own_bias, other_bias = weight_product(x_keeps[layer], d_parts[layer], packed)
-        weight_grads[layer] = own + other_core(other)
+        weight_grad = join(own, other_core(other), layer, layers, weight_grad)
         bias_grads[layer] = (own_bias + other_core(other_bias))[0]
-    weight_grad, bias_grad = jnp.stack(weight_grads), jnp.stack(bias_grads)
+    bias_grad = jnp.stack(bias_grads)
     own, other = table_product(counts, arrived)
     table_grad = own + other_core(other)
 

time: 218 us -> 226 us (1.037)
  other arithmetic: 14.5 us -> 8.97 us
  waiting for transfers between devices: 35.2 us -> 40.1 us
  Pallas kernels: 25 us -> 29.8 us
  starting transfers between devices: 93.3 us -> 97.3 us
    all_to_all x7, waiting for transfers between devices: 8.48 us -> 15.8 us  [swap(): return lax.all_to_all(pieces, axis, 0, 0, tiled=True)]
    ppermute x7, starting transfers between devices: 26.8 us -> 33.3 us  [other_core(): return lax.ppermute(value, 's', [(0, 1), (1, 0)])]
    another operation x4 -> x1, other arithmetic: 6.14 us -> 0.59 us  [body(): bias_grad = jnp.stack(bias_grads)]
    pallas_call x0 -> x2, Pallas kernels: none -> 4.69 us  [join(): pl.pallas_call(join_kernel, grid=(1,), in_specs=[whole(own.shape)] * 2 +...]
    all_to_all x7, starting transfers between devices: 41.7 us -> 39.2 us  [swap(): return lax.all_to_all(pieces, axis, 0, 0, tiled=True)]
    unnamed x65 -> x71, local copies, waits for them, and re-layouts: 20.3 us -> 19.7 us
  transfers between devices with their start and end apart: 35 -> 35, of which waited for: 15 -> 15; matrix products, arithmetic and copies ran while one was open for 8% -> 5% of each run, Pallas kernels for 9% -> 11%
where the time goes in v1:
time: 226 us; the launch traced here: 224 us
  starting transfers between devices  97.3 us (43%)
  waiting for transfers between devices  40.1 us (18%)
  Pallas kernels  29.8 us (13%)
  blocking collectives  24.8 us (11%)
  local copies, waits for them, and re-layouts  21.9 us (10%)
  other arithmetic  8.97 us (4%)
    all_to_all x7, starting transfers between devices, swap(): return lax.all_to_all(pieces, axis, 0, 0, tiled=True)  39.2 us
    ppermute x7, starting transfers between devices, other_core(): return lax.ppermute(value, 's', [(0, 1), (1, 0)])  33.3 us
    all_to_all x2, blocking collectives, swap(): return lax.all_to_all(pieces, axis, 0, 0, tiled=True)  24.8 us
    ppermute x21, starting transfers between devices, shift_in(): return lax.ppermute(value, axis, [(i, (i + k) % 4) for i in range(4)])  24.8 us
    ppermute x21, waiting for transfers between devices, shift_in(): return lax.ppermute(value, axis, [(i, (i + k) % 4) for i in range(4)])  24.3 us
    unnamed x71, local copies, waits for them, and re-layouts  19.7 us
    pallas_call x14, Pallas kernels, call(): pl.pallas_call(kernel, grid=(1,), in_specs=specs + [FREE] * len(earlier),...  17.5 us
    all_to_all x7, waiting for transfers between devices, swap(): return lax.all_to_all(pieces, axis, 0, 0, tiled=True)  15.8 us
  transfers between devices with their start and end apart: 35, of which 15 were waited for; matrix products, arithmetic and copies ran while one was open for 5% of the time, Pallas kernels for 11%

profile of v1, /device:TPU:1, one launch (start us, length us, event | category | flops | bytes accessed | tf_op | source)
XLA Modules:
  0.0 224.1 jit_solution(15388767792633494262)
XLA Ops:
  0.6 3.3 %collective-permute-start = (bf16[4,128,256]{2,1,0:T(8,128)(2,1)}, bf16[4,128,256]{2,1,0:T(8,128)(2,1)S(1)}, u32[]{:S(2)}, u32[]{:S(2)}) collective-permute-start(bf16[4,128,256]{2,1,0:T(8,128)(2,1)} %own_ref.1), channel_id=1, source_target_pairs={{0,128},{128,0},{1,129},{129,1},{2,130},{130,2},{3,131},{131,3},{4... | collective-permute-start | bytes 786440 | tf_op jit(solution)/shard_map/ppermute | solution.py:26
  6.3 2.2 collective-permute-start.5
  10.6 3.5 %count.1.counts_ref = bf16[4,256,512]{2,1,0:T(8,128)(2,1)S(1)} custom-call(f32[4,32,512]{2,1,0:T(8,128)S(1)} %fusion.ids_ref), custom_call_target="tpu_custom_call" | custom-call | tf_op jit(solution)/shard_map/count/pallas_call | solution.py:94
  18.1 2.4 %collective-permute-start.2 = (bf16[256,512]{1,0:T(8,128)(2,1)}, bf16[256,512]{1,0:T(8,128)(2,1)}, u32[]{:S(2)}, u32[]{:S(2)}) collective-permute-start(bf16[256,512]{1,0:T(8,128)(2,1)} %get-tuple-element.33), channel_id=1, source_target_pairs={{0,16},{8,24},{16,0},{24,8},{1,17},{9,25},{17,1},{25,9},{2,18},{10... | collective-permute-start | bytes 786440 | tf_op jit(solution)/shard_map/ppermute | solution.py:30
  22.1 11.4 %all_to_all.45 = bf16[16,2,1024]{2,1,0:T(2,128)(2,1)S(1)} all-to-all(bf16[16,2,1024]{2,1,0:T(2,128)(2,1)S(1)} %reshape.42), channel_id=1, replica_groups=mesh['s'=2,'y'=4,'x'=4,'z'=8] {'x','y'}, dimensions={0} | all-to-all | bytes 131072 | tf_op jit(solution)/shard_map/all_to_all | solution.py:34
  37.2 4.0 %all-to-all-start.1 = ((bf16[4,64,512]{2,1,0:T(8,128)(2,1)}), bf16[4,64,512]{2,1,0:T(8,128)(2,1)}, u32[]{:S(2)}, u32[]{:S(2)}) async-start(bf16[4,64,512]{2,1,0:T(8,128)(2,1)} %bitcast.18), calls=%async_computation.1 | async-start | bytes 524288 | tf_op jit(solution)/shard_map/all_to_all | solution.py:34
  43.3 3.5 %all-to-all-done.1 = bf16[4,64,512]{2,1,0:T(8,128)(2,1)} async-done(((bf16[4,64,512]{2,1,0:T(8,128)(2,1)}), bf16[4,64,512]{2,1,0:T(8,128)(2,1)}, u32[]{:S(2)}, u32[]{:S(2)}) %all-to-all-start.1) | async-done | bytes 262176 | tf_op jit(solution)/shard_map/all_to_all | solution.py:34
  48.7 7.0 %all-to-all-start.2 = ((bf16[8,64,512]{2,1,0:T(8,128)(2,1)}), bf16[8,64,512]{2,1,0:T(8,128)(2,1)}, u32[]{:S(2)}, u32[]{:S(2)}) async-start(bf16[8,64,512]{2,1,0:T(8,128)(2,1)} %copy-done.10), calls=%async_computation.2 | async-start | bytes 1048576 | tf_op jit(solution)/shard_map/all_to_all | solution.py:34
  58.9 2.1 collective-permute-done.8.refs_1_
  64.2 3.4 %collective-permute-start.12 = (bf16[256,512]{1,0:T(8,128)(2,1)S(1)}, bf16[256,512]{1,0:T(8,128)(2,1)S(1)}, u32[]{:S(2)}, u32[]{:S(2)}) collective-permute-start(bf16[256,512]{1,0:T(8,128)(2,1)S(1)} %collect.1.refs_0_), channel_id=1, source_target_pairs={{0,16},{8,24},{16,0},{24,8},{1,17},{9,25},{17,1},{25,9},{2,18},{10... | collective-permute-start | bytes 786440 | tf_op jit(solution)/shard_map/ppermute | solution.py:30
  67.6 2.6 %collective-permute-done.11.refs_1_ = bf16[256,512]{1,0:T(8,128)(2,1)S(1)} collective-permute-done((bf16[256,512]{1,0:T(8,128)(2,1)S(1)}, bf16[256,512]{1,0:T(8,128)(2,1)S(1)}, u32[]{:S(2)}, u32[]{:S(2)}) %collective-permute-start.11) | collective-permute-done | bytes 262176 | tf_op jit(solution)/shard_map/ppermute | solution.py:30
  70.2 5.5 %collective-permute-done.12.refs_2_ = bf16[256,512]{1,0:T(8,128)(2,1)S(1)} collective-permute-done((bf16[256,512]{1,0:T(8,128)(2,1)S(1)}, bf16[256,512]{1,0:T(8,128)(2,1)S(1)}, u32[]{:S(2)}, u32[]{:S(2)}) %collective-permute-start.12) | collective-permute-done | bytes 262176 | tf_op jit(solution)/shard_map/ppermute | solution.py:30
  78.8 6.7 %all-to-all-start.3 = ((bf16[8,64,512]{2,1,0:T(8,128)(2,1)}), bf16[8,64,512]{2,1,0:T(8,128)(2,1)}, u32[]{:S(2)}, u32[]{:S(2)}) async-start(bf16[8,64,512]{2,1,0:T(8,128)(2,1)} %after.2.refs_0_), calls=%async_computation.3 | async-start | bytes 1048576 | tf_op jit(solution)/shard_map/all_to_all | solution.py:34
  86.6 2.5 %backward_product.2 = (bf16[256,512]{1,0:T(8,128)(2,1)S(1)}, bf16[256,512]{1,0:T(8,128)(2,1)}, bf16[256,512]{1,0:T(8,128)(2,1)}, bf16[256,512]{1,0:T(8,128)(2,1)}) custom-call(s32[3]{0:T(128)S(1)} %pad_add_fusion.at_ref, bf16[8,64,512]{2,1,0:T(8,128)(2,1)} %all-to-all-done.2.refs_1_.d_ref, bf16[4,2,64,1024]{3,2,1,0:T(8,128)(2,1)S(1)} %stack_from.1.refs_4_.own_ref, ...), custom_call_target="tpu_custom_call" | custom-call | tf_op jit(solution)/shard_map/backward_product/pallas_call | solution.py:47
  89.9 2.7 %collective-permute-start.15 = (bf16[256,512]{1,0:T(8,128)(2,1)}, bf16[256,512]{1,0:T(8,128)(2,1)}, u32[]{:S(2)}, u32[]{:S(2)}) collective-permute-start(bf16[256,512]{1,0:T(8,128)(2,1)} %get-tuple-element.38), channel_id=1, source_target_pairs={{0,16},{8,24},{16,0},{24,8},{1,17},{9,25},{17,1},{25,9},{2,18},{10... | collective-permute-start | bytes 786440 | tf_op jit(solution)/shard_map/ppermute | solution.py:30
  92.5 5.1 %all-to-all-done.3 = bf16[8,64,512]{2,1,0:T(8,128)(2,1)} async-done(((bf16[8,64,512]{2,1,0:T(8,128)(2,1)}), bf16[8,64,512]{2,1,0:T(8,128)(2,1)}, u32[]{:S(2)}, u32[]{:S(2)}) %all-to-all-start.3) | async-done | bytes 524320 | tf_op jit(solution)/shard_map/all_to_all | solution.py:34
  102.7 13.4 %all_to_all.46.d_ref = bf16[4,4,64,512]{3,2,1,0:T(8,128)(2,1)S(1)} all-to-all(bf16[4,4,64,512]{3,2,1,0:T(8,128)(2,1)S(1)} %add_with.2), channel_id=1, replica_groups=mesh['s'=2,'y'=4,'x'=4,'z'=8] {'y'}, dimensions={0} | all-to-all | bytes 2097152 | tf_op jit(solution)/shard_map/all_to_all | solution.py:34
  118.7 6.6 %all-to-all-start.5 = ((bf16[8,64,512]{2,1,0:T(8,128)(2,1)}), bf16[8,64,512]{2,1,0:T(8,128)(2,1)}, u32[]{:S(2)}, u32[]{:S(2)}) async-start(bf16[8,64,512]{2,1,0:T(8,128)(2,1)} %copy-done.11), calls=%async_computation.5 | async-start | bytes 1048576 | tf_op jit(solution)/shard_map/all_to_all | solution.py:34
  126.4 3.1 %collective-permute-start.18 = (bf16[256,512]{1,0:T(8,128)(2,1)S(1)}, bf16[256,512]{1,0:T(8,128)(2,1)S(1)}, u32[]{:S(2)}, u32[]{:S(2)}) collective-permute-start(bf16[256,512]{1,0:T(8,128)(2,1)S(1)} %bitcast.64), channel_id=1, source_target_pairs={{0,16},{8,24},{16,0},{24,8},{1,17},{9,25},{17,1},{25,9},{2,18},{10... | collective-permute-start | bytes 786440 | tf_op jit(solution)/shard_map/ppermute | solution.py:30
  129.4 3.3 %collective-permute-done.17.refs_1_ = bf16[256,512]{1,0:T(8,128)(2,1)S(1)} collective-permute-done((bf16[256,512]{1,0:T(8,128)(2,1)S(1)}, bf16[256,512]{1,0:T(8,128)(2,1)S(1)}, u32[]{:S(2)}, u32[]{:S(2)}) %collective-permute-start.17) | collective-permute-done | bytes 262176 | tf_op jit(solution)/shard_map/ppermute | solution.py:30
  132.8 3.2 %collective-permute-done.18.refs_2_ = bf16[256,512]{1,0:T(8,128)(2,1)S(1)} collective-permute-done((bf16[256,512]{1,0:T(8,128)(2,1)S(1)}, bf16[256,512]{1,0:T(8,128)(2,1)S(1)}, u32[]{:S(2)}, u32[]{:S(2)}) %collective-permute-start.18) | collective-permute-done | bytes 262176 | tf_op jit(solution)/shard_map/ppermute | solution.py:30
  139.3 7.0 %all-to-all-start.6 = ((bf16[8,64,512]{2,1,0:T(8,128)(2,1)}), bf16[8,64,512]{2,1,0:T(8,128)(2,1)}, u32[]{:S(2)}, u32[]{:S(2)}) async-start(bf16[8,64,512]{2,1,0:T(8,128)(2,1)} %after.3.refs_0_), calls=%async_computation.6 | async-start | bytes 1048576 | tf_op jit(solution)/shard_map/all_to_all | solution.py:34
  150.1 3.6 %collective-permute-start.21 = (bf16[256,512]{1,0:T(8,128)(2,1)S(1)}, bf16[256,512]{1,0:T(8,128)(2,1)S(1)}, u32[]{:S(2)}, u32[]{:S(2)}) collective-permute-start(bf16[256,512]{1,0:T(8,128)(2,1)S(1)} %get-tuple-element.43), channel_id=1, source_target_pairs={{0,16},{8,24},{16,0},{24,8},{1,17},{9,25},{17,1},{25,9},{2,18},{10... | collective-permute-start | bytes 786440 | tf_op jit(solution)/shard_map/ppermute | solution.py:30
  153.6 2.9 %collective-permute-done.20.refs_0_.refs_1_ = bf16[256,512]{1,0:T(8,128)(2,1)S(1)} collective-permute-done((bf16[256,512]{1,0:T(8,128)(2,1)S(1)}, bf16[256,512]{1,0:T(8,128)(2,1)S(1)}, u32[]{:S(2)}, u32[]{:S(2)}) %collective-permute-start.20) | collective-permute-done | bytes 262176 | tf_op jit(solution)/shard_map/ppermute | solution.py:30
  162.3 3.6 %all-to-all-start.7 = ((bf16[4,3,64,512]{3,2,1,0:T(8,128)(2,1)}), bf16[4,3,64,512]{3,2,1,0:T(8,128)(2,1)S(1)}, u32[]{:S(2)}, u32[]{:S(2)}) async-start(bf16[4,3,64,512]{3,2,1,0:T(8,128)(2,1)} %copy-done.9), calls=%async_computation.7 | async-start | bytes 1572864 | tf_op jit(solution)/shard_map/all_to_all | solution.py:34
  167.0 7.2 %all-to-all-done.7.d_ref = bf16[4,3,64,512]{3,2,1,0:T(8,128)(2,1)S(1)} async-done(((bf16[4,3,64,512]{3,2,1,0:T(8,128)(2,1)}), bf16[4,3,64,512]{3,2,1,0:T(8,128)(2,1)S(1)}, u32[]{:S(2)}, u32[]{:S(2)}) %all-to-all-start.7) | async-done | bytes 786464 | tf_op jit(solution)/shard_map/all_to_all | solution.py:34
  176.5 4.1 %all-to-all-start.8 = ((bf16[16,64,640]{2,1,0:T(8,128)(2,1)}), bf16[16,64,640]{2,1,0:T(8,128)(2,1)S(1)}, u32[]{:S(2)}, u32[]{:S(2)}) async-start(bf16[16,64,640]{2,1,0:T(8,128)(2,1)} %pack.1.refs_0_), calls=%async_computation.8 | async-start | bytes 2621440 | tf_op jit(solution)/shard_map/all_to_all | solution.py:34
  180.6 18.8 %collective-permute-start.25 = (f32[1024,256]{1,0:T(8,128)}, f32[1024,256]{1,0:T(8,128)}, u32[]{:S(2)}, u32[]{:S(2)}) collective-permute-start(f32[1024,256]{1,0:T(8,128)} %copy-done.27), channel_id=1, source_target_pairs={{0,128},{128,0},{1,129},{129,1},{2,130},{130,2},{3,131},{131,3},{4... | collective-permute-start | bytes 3145736 | tf_op jit(solution)/shard_map/ppermute | solution.py:26
  200.5 2.6 %weight_product.3 = (f32[1024,256]{1,0:T(8,128)S(1)}, f32[1024,256]{1,0:T(8,128)}, f32[8,256]{1,0:T(8,128)S(1)}, f32[8,256]{1,0:T(8,128)S(1)}) custom-call(bf16[4,256,512]{2,1,0:T(8,128)(2,1)S(1)} %copy-done.13, bf16[4,3,64,512]{3,2,1,0:T(8,128)(2,1)S(1)} %all-to-all-done.7.d_ref, bf16[16,64,640]{2,1,0:T(8,128)(2,1)} %pack.1.refs_0_), custom_call_target="tpu_custom_call" | custom-call | tf_op jit(solution)/shard_map/weight_product/pallas_call | solution.py:215
  206.3 8.8 %collective-permute-start.23 = (f32[4,128,256]{2,1,0:T(8,128)}, f32[4,128,256]{2,1,0:T(8,128)}, u32[]{:S(2)}, u32[]{:S(2)}) collective-permute-start(f32[4,128,256]{2,1,0:T(8,128)} %get-tuple-element.48), channel_id=1, source_target_pairs={{0,128},{128,0},{1,129},{129,1},{2,130},{130,2},{3,131},{131,3},{4... | collective-permute-start | bytes 1572872 | tf_op jit(solution)/shard_map/ppermute | solution.py:26
  215.1 2.4 %join.2.refs_0_ = f32[2,1024,256]{2,1,0:T(8,128)} custom-call(f32[1024,256]{1,0:T(8,128)S(1)} %copy-done.8, f32[1024,256]{1,0:T(8,128)} %collective-permute-done.25.other_ref), custom_call_target="tpu_custom_call" | custom-call | tf_op jit(solution)/shard_map/join/pallas_call | solution.py:235
  218.1 2.3 %join.3 = f32[2,1024,256]{2,1,0:T(8,128)} custom-call(f32[1024,256]{1,0:T(8,128)S(1)} %copy-done.17, f32[1024,256]{1,0:T(8,128)} %collective-permute-done.24.other_ref, f32[2,1024,256]{2,1,0:T(8,128)} %join.2.refs_0_), custom_call_target="tpu_custom_call", output_to_operand_aliasing={{}: (2, {})} | custom-call | tf_op jit(solution)/shard_map/join/pallas_call | solution.py:235
  (156 shorter events, 61.9 us)
Async XLA Ops:
  0.6 13.6 %collective-permute-start = (bf16[4,128,256]{2,1,0:T(8,128)(2,1)}, bf16[4,128,256]{2,1,0:T(8,128)(2,1)S(1)}, u32[]{:S(2)}, u32[]{:S(2)}) collective-permute-start(bf16[4,128,256]{2,1,0:T(8,128)(2,1)} %own_ref.1), channel_id=1, source_target_pairs={{0,128},{128,0},{1,129},{129,1},{2,130},{130,2},{3,131},{131,3},{4... | collective-permute-start | bytes 786440 | tf_op jit(solution)/shard_map/ppermute | solution.py:26
  6.3 14.3 %collective-permute-start.4 = (bf16[2,64,1024]{2,1,0:T(8,128)(2,1)}, bf16[2,64,1024]{2,1,0:T(8,128)(2,1)S(1)}, u32[]{:S(2)}, u32[]{:S(2)}) collective-permute-start(bf16[2,64,1024]{2,1,0:T(8,128)(2,1)} %get-tuple-element.73), channel_id=1, source_target_pairs={{0,32},{32,64},{64,96},{96,0},{1,33},{33,65},{65,97},{97,1},{2,34}... | collective-permute-start | bytes 786440 | tf_op jit(solution)/shard_map/ppermute | solution.py:30
  6.3 27.3 %collective-permute-start.5 = (bf16[2,64,1024]{2,1,0:T(8,128)(2,1)S(1)}, bf16[2,64,1024]{2,1,0:T(8,128)(2,1)S(1)}, u32[]{:S(2)}, u32[]{:S(2)}) collective-permute-start(bf16[2,64,1024]{2,1,0:T(8,128)(2,1)S(1)} %get-tuple-element.72), channel_id=1, source_target_pairs={{0,64},{32,96},{64,0},{96,32},{1,65},{33,97},{65,1},{97,33},{2,66}... | collective-permute-start | bytes 786440 | tf_op jit(solution)/shard_map/ppermute | solution.py:30
  8.5 25.2 %collective-permute-start.6 = (bf16[2,64,1024]{2,1,0:T(8,128)(2,1)S(1)}, bf16[2,64,1024]{2,1,0:T(8,128)(2,1)S(1)}, u32[]{:S(2)}, u32[]{:S(2)}) collective-permute-start(bf16[2,64,1024]{2,1,0:T(8,128)(2,1)S(1)} %get-tuple-element.71), channel_id=1, source_target_pairs={{0,96},{32,0},{64,32},{96,64},{1,97},{33,1},{65,33},{97,65},{2,98}... | collective-permute-start | bytes 786440 | tf_op jit(solution)/shard_map/ppermute | solution.py:30
  16.9 17.4 %collective-permute-start.1 = (bf16[256,512]{1,0:T(8,128)(2,1)}, bf16[256,512]{1,0:T(8,128)(2,1)}, u32[]{:S(2)}, u32[]{:S(2)}) collective-permute-start(bf16[256,512]{1,0:T(8,128)(2,1)} %get-tuple-element.32), channel_id=1, source_target_pairs={{0,8},{8,16},{16,24},{24,0},{1,9},{9,17},{17,25},{25,1},{2,10},{10... | collective-permute-start | bytes 786440 | tf_op jit(solution)/shard_map/ppermute | solution.py:30
  18.1 16.2 %collective-permute-start.2 = (bf16[256,512]{1,0:T(8,128)(2,1)}, bf16[256,512]{1,0:T(8,128)(2,1)}, u32[]{:S(2)}, u32[]{:S(2)}) collective-permute-start(bf16[256,512]{1,0:T(8,128)(2,1)} %get-tuple-element.33), channel_id=1, source_target_pairs={{0,16},{8,24},{16,0},{24,8},{1,17},{9,25},{17,1},{25,9},{2,18},{10... | collective-permute-start | bytes 786440 | tf_op jit(solution)/shard_map/ppermute | solution.py:30
  20.6 13.7 %collective-permute-start.3 = (bf16[256,512]{1,0:T(8,128)(2,1)}, bf16[256,512]{1,0:T(8,128)(2,1)}, u32[]{:S(2)}, u32[]{:S(2)}) collective-permute-start(bf16[256,512]{1,0:T(8,128)(2,1)} %get-tuple-element.34), channel_id=1, source_target_pairs={{0,24},{8,0},{16,8},{24,16},{1,25},{9,1},{17,9},{25,17},{2,26},{10... | collective-permute-start | bytes 786440 | tf_op jit(solution)/shard_map/ppermute | solution.py:30
  37.2 9.6 %all-to-all-start.1 = ((bf16[4,64,512]{2,1,0:T(8,128)(2,1)}), bf16[4,64,512]{2,1,0:T(8,128)(2,1)}, u32[]{:S(2)}, u32[]{:S(2)}) async-start(bf16[4,64,512]{2,1,0:T(8,128)(2,1)} %bitcast.18), calls=%async_computation.1 | async-start | bytes 524288 | tf_op jit(solution)/shard_map/all_to_all | solution.py:34
  41.4 34.3 %collective-permute-start.7 = (bf16[4,2,64,1024]{3,2,1,0:T(8,128)(2,1)S(1)}, bf16[4,2,64,1024]{3,2,1,0:T(8,128)(2,1)S(1)}, u32[]{:S(2)}, u32[]{:S(2)}) collective-permute-start(bf16[4,2,64,1024]{3,2,1,0:T(8,128)(2,1)S(1)} %stack_from.1.refs_4_.own_ref), channel_id=1, source_target_pairs={{0,128},{128,0},{1,129},{129,1},{2,130},{130,2},{3,131},{131,3},{4... | collective-permute-start | bytes 3145736 | tf_op jit(solution)/shard_map/ppermute | solution.py:26
  48.7 30.1 %all-to-all-start.2 = ((bf16[8,64,512]{2,1,0:T(8,128)(2,1)}), bf16[8,64,512]{2,1,0:T(8,128)(2,1)}, u32[]{:S(2)}, u32[]{:S(2)}) async-start(bf16[8,64,512]{2,1,0:T(8,128)(2,1)} %copy-done.10), calls=%async_computation.2 | async-start | bytes 1048576 | tf_op jit(solution)/shard_map/all_to_all | solution.py:34
  62.4 7.8 %collective-permute-start.11 = (bf16[256,512]{1,0:T(8,128)(2,1)S(1)}, bf16[256,512]{1,0:T(8,128)(2,1)S(1)}, u32[]{:S(2)}, u32[]{:S(2)}) collective-permute-start(bf16[256,512]{1,0:T(8,128)(2,1)S(1)} %collect.1.refs_0_), channel_id=1, source_target_pairs={{0,8},{8,16},{16,24},{24,0},{1,9},{9,17},{17,25},{25,1},{2,10},{10... | collective-permute-start | bytes 786440 | tf_op jit(solution)/shard_map/ppermute | solution.py:30
  64.2 11.5 %collective-permute-start.12 = (bf16[256,512]{1,0:T(8,128)(2,1)S(1)}, bf16[256,512]{1,0:T(8,128)(2,1)S(1)}, u32[]{:S(2)}, u32[]{:S(2)}) collective-permute-start(bf16[256,512]{1,0:T(8,128)(2,1)S(1)} %collect.1.refs_0_), channel_id=1, source_target_pairs={{0,16},{8,24},{16,0},{24,8},{1,17},{9,25},{17,1},{25,9},{2,18},{10... | collective-permute-start | bytes 786440 | tf_op jit(solution)/shard_map/ppermute | solution.py:30
  67.6 8.1 %collective-permute-start.13 = (bf16[256,512]{1,0:T(8,128)(2,1)S(1)}, bf16[256,512]{1,0:T(8,128)(2,1)S(1)}, u32[]{:S(2)}, u32[]{:S(2)}) collective-permute-start(bf16[256,512]{1,0:T(8,128)(2,1)S(1)} %collect.1.refs_0_), channel_id=1, source_target_pairs={{0,24},{8,0},{16,8},{24,16},{1,25},{9,1},{17,9},{25,17},{2,26},{10... | collective-permute-start | bytes 786440 | tf_op jit(solution)/shard_map/ppermute | solution.py:30
  78.8 18.9 %all-to-all-start.3 = ((bf16[8,64,512]{2,1,0:T(8,128)(2,1)}), bf16[8,64,512]{2,1,0:T(8,128)(2,1)}, u32[]{:S(2)}, u32[]{:S(2)}) async-start(bf16[8,64,512]{2,1,0:T(8,128)(2,1)} %after.2.refs_0_), calls=%async_computation.3 | async-start | bytes 1048576 | tf_op jit(solution)/shard_map/all_to_all | solution.py:34
  89.9 9.0 %collective-permute-start.14 = (bf16[256,512]{1,0:T(8,128)(2,1)}, bf16[256,512]{1,0:T(8,128)(2,1)}, u32[]{:S(2)}, u32[]{:S(2)}) collective-permute-start(bf16[256,512]{1,0:T(8,128)(2,1)} %get-tuple-element.37), channel_id=1, source_target_pairs={{0,8},{8,16},{16,24},{24,0},{1,9},{9,17},{17,25},{25,1},{2,10},{10... | collective-permute-start | bytes 786440 | tf_op jit(solution)/shard_map/ppermute | solution.py:30
  89.9 9.8 %collective-permute-start.15 = (bf16[256,512]{1,0:T(8,128)(2,1)}, bf16[256,512]{1,0:T(8,128)(2,1)}, u32[]{:S(2)}, u32[]{:S(2)}) collective-permute-start(bf16[256,512]{1,0:T(8,128)(2,1)} %get-tuple-element.38), channel_id=1, source_target_pairs={{0,16},{8,24},{16,0},{24,8},{1,17},{9,25},{17,1},{25,9},{2,18},{10... | collective-permute-start | bytes 786440 | tf_op jit(solution)/shard_map/ppermute | solution.py:30
  92.5 7.8 %collective-permute-start.16 = (bf16[256,512]{1,0:T(8,128)(2,1)}, bf16[256,512]{1,0:T(8,128)(2,1)}, u32[]{:S(2)}, u32[]{:S(2)}) collective-permute-start(bf16[256,512]{1,0:T(8,128)(2,1)} %get-tuple-element.39), channel_id=1, source_target_pairs={{0,24},{8,0},{16,8},{24,16},{1,25},{9,1},{17,9},{25,17},{2,26},{10... | collective-permute-start | bytes 786440 | tf_op jit(solution)/shard_map/ppermute | solution.py:30
  118.7 20.6 %all-to-all-start.5 = ((bf16[8,64,512]{2,1,0:T(8,128)(2,1)}), bf16[8,64,512]{2,1,0:T(8,128)(2,1)}, u32[]{:S(2)}, u32[]{:S(2)}) async-start(bf16[8,64,512]{2,1,0:T(8,128)(2,1)} %copy-done.11), calls=%async_computation.5 | async-start | bytes 1048576 | tf_op jit(solution)/shard_map/all_to_all | solution.py:34
  126.3 6.5 %collective-permute-start.17 = (bf16[256,512]{1,0:T(8,128)(2,1)S(1)}, bf16[256,512]{1,0:T(8,128)(2,1)S(1)}, u32[]{:S(2)}, u32[]{:S(2)}) collective-permute-start(bf16[256,512]{1,0:T(8,128)(2,1)S(1)} %bitcast.63), channel_id=1, source_target_pairs={{0,8},{8,16},{16,24},{24,0},{1,9},{9,17},{17,25},{25,1},{2,10},{10... | collective-permute-start | bytes 786440 | tf_op jit(solution)/shard_map/ppermute | solution.py:30
  126.4 9.6 %collective-permute-start.18 = (bf16[256,512]{1,0:T(8,128)(2,1)S(1)}, bf16[256,512]{1,0:T(8,128)(2,1)S(1)}, u32[]{:S(2)}, u32[]{:S(2)}) collective-permute-start(bf16[256,512]{1,0:T(8,128)(2,1)S(1)} %bitcast.64), channel_id=1, source_target_pairs={{0,16},{8,24},{16,0},{24,8},{1,17},{9,25},{17,1},{25,9},{2,18},{10... | collective-permute-start | bytes 786440 | tf_op jit(solution)/shard_map/ppermute | solution.py:30
  129.4 6.8 %collective-permute-start.19 = (bf16[256,512]{1,0:T(8,128)(2,1)S(1)}, bf16[256,512]{1,0:T(8,128)(2,1)S(1)}, u32[]{:S(2)}, u32[]{:S(2)}) collective-permute-start(bf16[256,512]{1,0:T(8,128)(2,1)S(1)} %bitcast.65), channel_id=1, source_target_pairs={{0,24},{8,0},{16,8},{24,16},{1,25},{9,1},{17,9},{25,17},{2,26},{10... | collective-permute-start | bytes 786440 | tf_op jit(solution)/shard_map/ppermute | solution.py:30
  139.3 20.9 %all-to-all-start.6 = ((bf16[8,64,512]{2,1,0:T(8,128)(2,1)}), bf16[8,64,512]{2,1,0:T(8,128)(2,1)}, u32[]{:S(2)}, u32[]{:S(2)}) async-start(bf16[8,64,512]{2,1,0:T(8,128)(2,1)} %after.3.refs_0_), calls=%async_computation.6 | async-start | bytes 1048576 | tf_op jit(solution)/shard_map/all_to_all | solution.py:34
  150.1 6.4 %collective-permute-start.20 = (bf16[256,512]{1,0:T(8,128)(2,1)S(1)}, bf16[256,512]{1,0:T(8,128)(2,1)S(1)}, u32[]{:S(2)}, u32[]{:S(2)}) collective-permute-start(bf16[256,512]{1,0:T(8,128)(2,1)S(1)} %get-tuple-element.42), channel_id=1, source_target_pairs={{0,8},{8,16},{16,24},{24,0},{1,9},{9,17},{17,25},{25,1},{2,10},{10... | collective-permute-start | bytes 786440 | tf_op jit(solution)/shard_map/ppermute | solution.py:30
  150.1 10.1 %collective-permute-start.21 = (bf16[256,512]{1,0:T(8,128)(2,1)S(1)}, bf16[256,512]{1,0:T(8,128)(2,1)S(1)}, u32[]{:S(2)}, u32[]{:S(2)}) collective-permute-start(bf16[256,512]{1,0:T(8,128)(2,1)S(1)} %get-tuple-element.43), channel_id=1, source_target_pairs={{0,16},{8,24},{16,0},{24,8},{1,17},{9,25},{17,1},{25,9},{2,18},{10... | collective-permute-start | bytes 786440 | tf_op jit(solution)/shard_map/ppermute | solution.py:30
  153.6 6.6 %collective-permute-start.22 = (bf16[256,512]{1,0:T(8,128)(2,1)S(1)}, bf16[256,512]{1,0:T(8,128)(2,1)S(1)}, u32[]{:S(2)}, u32[]{:S(2)}) collective-permute-start(bf16[256,512]{1,0:T(8,128)(2,1)S(1)} %get-tuple-element.44), channel_id=1, source_target_pairs={{0,24},{8,0},{16,8},{24,16},{1,25},{9,1},{17,9},{25,17},{2,26},{10... | collective-permute-start | bytes 786440 | tf_op jit(solution)/shard_map/ppermute | solution.py:30
  162.3 11.9 %all-to-all-start.7 = ((bf16[4,3,64,512]{3,2,1,0:T(8,128)(2,1)}), bf16[4,3,64,512]{3,2,1,0:T(8,128)(2,1)S(1)}, u32[]{:S(2)}, u32[]{:S(2)}) async-start(bf16[4,3,64,512]{3,2,1,0:T(8,128)(2,1)} %copy-done.9), calls=%async_computation.7 | async-start | bytes 1572864 | tf_op jit(solution)/shard_map/all_to_all | solution.py:34
  176.5 28.2 %all-to-all-start.8 = ((bf16[16,64,640]{2,1,0:T(8,128)(2,1)}), bf16[16,64,640]{2,1,0:T(8,128)(2,1)S(1)}, u32[]{:S(2)}, u32[]{:S(2)}) async-start(bf16[16,64,640]{2,1,0:T(8,128)(2,1)} %pack.1.refs_0_), calls=%async_computation.8 | async-start | bytes 2621440 | tf_op jit(solution)/shard_map/all_to_all | solution.py:34
  180.6 34.6 %collective-permute-start.25 = (f32[1024,256]{1,0:T(8,128)}, f32[1024,256]{1,0:T(8,128)}, u32[]{:S(2)}, u32[]{:S(2)}) collective-permute-start(f32[1024,256]{1,0:T(8,128)} %copy-done.27), channel_id=1, source_target_pairs={{0,128},{128,0},{1,129},{129,1},{2,130},{130,2},{3,131},{131,3},{4... | collective-permute-start | bytes 3145736 | tf_op jit(solution)/shard_map/ppermute | solution.py:26
  204.1 14.0 %collective-permute-start.24 = (f32[1024,256]{1,0:T(8,128)}, f32[1024,256]{1,0:T(8,128)}, u32[]{:S(2)}, u32[]{:S(2)}) collective-permute-start(f32[1024,256]{1,0:T(8,128)} %get-tuple-element.51), channel_id=1, source_target_pairs={{0,128},{128,0},{1,129},{129,1},{2,130},{130,2},{3,131},{131,3},{4... | collective-permute-start | bytes 3145736 | tf_op jit(solution)/shard_map/ppermute | solution.py:26
  204.2 10.9 %collective-permute-start.27 = (f32[8,256]{1,0:T(8,128)S(1)}, f32[8,256]{1,0:T(8,128)S(1)}, u32[]{:S(2)}, u32[]{:S(2)}) collective-permute-start(f32[8,256]{1,0:T(8,128)S(1)} %get-tuple-element.56), channel_id=1, source_target_pairs={{0,128},{128,0},{1,129},{129,1},{2,130},{130,2},{3,131},{131,3},{4... | collective-permute-start | bytes 24584 | tf_op jit(solution)/shard_map/ppermute | solution.py:26
  204.7 12.9 %collective-permute-start.26 = (f32[8,256]{1,0:T(8,128)S(1)}, f32[8,256]{1,0:T(8,128)S(1)}, u32[]{:S(2)}, u32[]{:S(2)}) collective-permute-start(f32[8,256]{1,0:T(8,128)S(1)} %get-tuple-element.54), channel_id=1, source_target_pairs={{0,128},{128,0},{1,129},{129,1},{2,130},{130,2},{3,131},{131,3},{4... | collective-permute-start | bytes 24584 | tf_op jit(solution)/shard_map/ppermute | solution.py:26
  206.3 16.0 %collective-permute-start.23 = (f32[4,128,256]{2,1,0:T(8,128)}, f32[4,128,256]{2,1,0:T(8,128)}, u32[]{:S(2)}, u32[]{:S(2)}) collective-permute-start(f32[4,128,256]{2,1,0:T(8,128)} %get-tuple-element.48), channel_id=1, source_target_pairs={{0,128},{128,0},{1,129},{129,1},{2,130},{130,2},{3,131},{131,3},{4... | collective-permute-start | bytes 1572872 | tf_op jit(solution)/shard_map/ppermute | solution.py:26
  (36 other events, 291.4 us)
